TPU v7x, 512 devices: a whole 4x8x8 slice. The times are simulated.
512 devices in a mesh: section: 16 (over z, core), tensor: 32 (over y, x).
Axes of the slice: x: 4, y: 8, z: 8, core: 2. Of those that a mesh axis runs over, the one named last changes fastest.
Arguments:
- resid: bfloat16 [128, 3584], P('tensor'), may hold values from -6 to 6
- w_enc: bfloat16 [114688, 3584], P(('section', 'tensor')), may hold values from -0.09375 to 0.09375
- b_enc: float32 [114688], P(('section', 'tensor')), may hold values from -1 to 0.5
- w_dec: bfloat16 [114688, 3584], P(('section', 'tensor')), may hold values from -0.015625 to 0.015625
- b_dec: float32 [3584], replicated, may hold values from -3 to 3
Outputs:
- recon: float32 [128, 3584], P('tensor')
- grad_w_dec: bfloat16 [114688, 3584], P(('section', 'tensor'))
- code_grad: float32 [128, 114688], P(None, ('section', 'tensor'))
- grad_b_dec: float32 [3584], replicated
- loss_value: float32 [], replicated
All inputs are finite; a program needn't handle non-finite values.
Results may differ from a plain program's by a relative error of at most 0.0032.
The roundings to bfloat16 on the way count: a program that leaves them out, or rounds other values in their place, can miss the bound.
Values may be sent and summed in bfloat16 or wider, within the bound.
A program may use at most 64 MiB of HBM per device.

v0:
```python
import jax
import jax.numpy as jnp
from jax import lax
from jax.sharding import PartitionSpec as P

epsilon = 1e-06


def per_device(resid, w_enc, b_enc, w_dec, b_dec):
    stream = lax.all_gather(resid, "tensor", axis=0, tiled=True)
    preact = (
        lax.dot_general(stream, w_enc, (((1,), (1,)), ((), ())), preferred_element_type=jnp.float32)
        + b_enc
    )
    codes = jnp.maximum(preact, 0.0).astype(jnp.bfloat16)
    codes_f32 = codes.astype(jnp.float32)
    dec_f32 = w_dec.astype(jnp.float32)
    dec_norm = jnp.sqrt(jnp.sum(dec_f32 * dec_f32, axis=1) + epsilon)
    penalty = lax.psum(jnp.sum(codes_f32 * dec_norm), ("section", "tensor"))
    own_rows = resid.shape[0]
    total_rows = stream.shape[0]
    model_width = stream.shape[1]
    partial_value = jnp.dot(codes, w_dec, preferred_element_type=jnp.float32)
    summed = lax.psum(partial_value, ("section", "tensor"))
    recon_all = summed + b_dec
    errors = recon_all - stream.astype(jnp.float32)
    first_row = lax.axis_index("tensor") * own_rows
    recon = lax.dynamic_slice_in_dim(recon_all, first_row, own_rows, 0)
    squares = jnp.sum(errors * errors)
    grad_b_dec = jnp.sum(errors, axis=0)
    err_half = errors.astype(jnp.bfloat16)
    loss_value = (0.5 * squares + penalty) / (total_rows * model_width)
    code_sums = jnp.sum(codes_f32, axis=0)
    grad_w_dec = lax.dot_general(
        codes, err_half, (((0,), (0,)), ((), ())), preferred_element_type=jnp.float32
    )
    grad_w_dec = grad_w_dec + code_sums[:, None] * dec_f32 / dec_norm[:, None]
    code_grad = (
        lax.dot_general(
            err_half, w_dec, (((1,), (1,)), ((), ())), preferred_element_type=jnp.float32
        )
        + dec_norm
    )
    return (recon, grad_w_dec.astype(jnp.bfloat16), code_grad, grad_b_dec, loss_value)


def solution(mesh):
    in_specs = (
        P("tensor", None),
        P(("section", "tensor"), None),
        P(("section", "tensor")),
        P(("section", "tensor"), None),
        P(),
    )
    out_specs = (
        P("tensor", None),
        P(("section", "tensor"), None),
        P(None, ("section", "tensor")),
        P(),
        P(),
    )
    return jax.shard_map(
        per_device, mesh=mesh, in_specs=in_specs, out_specs=out_specs, check_vma=False
    )
```

profile of v0, /device:TPU:1, one launch (start us, length us, event | category | flops | bytes accessed | tf_op | source)
XLA Modules:
  0.0 361.0 jit_solution(16243876525081524570)
XLA Ops:
  7.2 0.0 copy-start
  7.2 0.0 all-reduce.2.cloned.1.call-start
  7.2 40.3 %all-gather = bf16[32,4,3584]{2,1,0:T(4,128)(2,1)S(1)} all-gather(bf16[1,4,3584]{2,1,0:T(4,128)(2,1)} %bitcast.7), channel_id=1, replica_groups=mesh['section'=16,'tensor'=32] {'tensor'}, dimensions={0}, use_global_device_ids=true | all-gather | bytes 946176 | tf_op jit(solution)/shard_map/all_gather | solution.py:10
  47.5 0.0 copy-start.4
  47.5 0.2 reshape.22
  47.7 0.0 copy-start.1
  47.7 1.9 fusion.2
  49.7 0.0 copy-done
  49.7 0.0 copy-done.4
  49.7 1.2 fusion.7
  50.9 0.0 copy-done.1
  50.9 0.0 copy-start.3
  50.9 1.7 fusion.10
  52.6 0.0 all-reduce.2.cloned.1.call-update
  52.6 114.0 %psum.15 = f32[]{:T(128)} all-reduce(f32[]{:T(128)} %get-tuple-element.7), channel_id=1, replica_groups=mesh['section'=16,'tensor'=32] {'section','tensor'}, use_global_device_ids=true, to_apply=%region_6.0 | all-reduce | flops 1 | bytes 8 | tf_op jit(solution)/shard_map/psum | solution.py:19
  166.6 178.5 %all-reduce.2.cloned.1.call-done = f32[128,3584]{1,0:T(8,128)} async-done(((f32[128,3584]{1,0:T(8,128)}), f32[128,3584]{1,0:T(8,128)}) %all-reduce.2.cloned.1.call-update) | async-done | bytes 1835024 | tf_op jit(solution)/shard_map/psum | solution.py:24
  345.2 0.0 copy-done.3
  345.2 0.0 copy-start.2
  345.2 2.8 multiply_reduce_fusion
  348.0 0.0 copy-done.2
  348.0 1.3 convolution_add_fusion.1
  349.3 1.9 fusion
  351.2 0.6 constant_dynamic-slice_fusion
  (1 shorter events, 0.0 us)
Async XLA Ops:
  7.2 42.5 %copy-start = (bf16[224,3584]{1,0:T(8,128)(2,1)S(1)}, bf16[224,3584]{1,0:T(8,128)(2,1)}, u32[]{:S(2)}) copy-start(bf16[224,3584]{1,0:T(8,128)(2,1)} %param.6) | copy-start | bytes 4816900
  7.2 338.0 %all-reduce.2.cloned.1.call-start = ((), (), s32[]{:S(2)}) async-start(), calls=%async_computation | async-start | bytes 3670016 | tf_op jit(solution)/shard_map/psum | solution.py:24
  47.5 2.2 copy-start.4
  47.7 3.2 copy-start.1
  50.9 294.3 %copy-start.3 = (f32[3584]{0:T(1024)S(1)}, f32[3584]{0:T(1024)}, u32[]{:S(2)}) copy-start(f32[3584]{0:T(1024)} %param.9) | copy-start | bytes 43012
  345.2 2.8 copy-start.2
Sparse Core Ops, SparseCore 0:
  52.7 292.4 all-reduce.1
where the time goes:
time: 361 us
  waiting for transfers between devices  179 us (50%)
  blocking collectives  154 us (43%)
  between operations  16.4 us (5%)
  matrix products  6.08 us (2%)
  other arithmetic  4.75 us (1%)
    psum x1, waiting for transfers between devices, per_device(): summed = lax.psum(partial_value, ('section', 'tensor'))  179 us
    psum x1, blocking collectives, per_device(): penalty = lax.psum(jnp.sum(codes_f32 * dec_norm), ('section', 'tensor'))  114 us
    all_gather x1, blocking collectives, per_device(): stream = lax.all_gather(resid, 'tensor', axis=0, tiled=True)  40.3 us
  transfers between devices with their start and end apart: 1, of which 1 were waited for; matrix products, arithmetic and copies ran while one was open for 0% of the time, Pallas kernels for 0%

commit v1 on v0

v1 whole, which is shorter than its diff:
```python
import functools

import jax
import jax.numpy as jnp
from jax import lax
from jax.experimental import pallas as pl
from jax.experimental.pallas import tpu as pltpu
from jax.sharding import PartitionSpec as P

MESH = pl.DeviceIdType.MESH
F32, BF16 = jnp.float32, jnp.bfloat16
epsilon = 1e-06

NX, NY, NZ = 4, 8, 8
D, LAT, ROWS = 3584, 224, 128
HALF, Q = D // 2, D // 4
SCALE = 1.0 / (ROWS * D)
NEAR = (1, 7, 2, 6, 3, 5, 4)
FAR = (4, 3, 5, 2, 6, 1, 7)


def far_step(n):
    return 4 + (1 - 2 * (n % 2)) * ((n + 1) // 2)


def near_step(n):
    return (1 - 2 * (n % 2)) * ((n + 2) // 2) + 8 * (n % 2)


def kernel(
    resid, wenc, benc, wdec, bdec,
    recon_o, gw_o, cg_o, gb_o, loss_o,
    rg, we, wd, wds, bs, lhs, px, pr, cc, part, got, mid, ups, zb, err, rc, gws,
    pbx, pby, pbz, pbc,
    load_sem, gy, gx, gsend, sib_send, sib_recv, pr_sem,
    rx, ry, rz, rsend, ey, ex, es, esend, rc_sem, pen_recv, pen_send, out_sem,
):
    section, tensor = lax.axis_index("section"), lax.axis_index("tensor")
    z, c = section // 2, section % 2
    y, x = tensor // 4, tensor % 4
    h, k = x % 2, x // 2

    def dev(xx, yy, zz, co):
        return (zz * 2 + co, yy * 4 + xx)

    def at_x(i):
        return dev((x + i) % NX, y, z, c)

    def at_y(j):
        return dev(x, (y + j) % NY, z, c)

    def at_z(j):
        return dev(x, y, (z + j) % NZ, c)

    sib = dev(x, y, z, 1 - c)

    def push(src, dst, ssem, rsem, to):
        copy = pltpu.make_async_remote_copy(src, dst, ssem, rsem, device_id=to, device_id_type=MESH)
        copy.start()
        return copy

    def took(ref, ssem, rsem):
        return pltpu.make_async_remote_copy(ref, ref, ssem, rsem, device_id=sib, device_id_type=MESH)

    own = pltpu.make_async_copy(
        resid.at[:, pl.ds(pl.multiple_of(c * HALF, 128), HALF)], rg.at[x, y], load_sem.at[0])
    own.start()
    enc_load = pltpu.make_async_copy(
        wenc.at[:, pl.ds(pl.multiple_of(c * HALF, 128), HALF)], we.at[0], load_sem.at[1])
    enc_load.start()
    dec_load = [
        pltpu.make_async_copy(wdec.at[:, q * Q:(q + 1) * Q], wd.at[q], load_sem.at[2 + q]) for q in range(4)
    ]
    for copy in dec_load:
        copy.start()

    barrier = pltpu.get_barrier_semaphore()
    partners = [at_x(i) for i in (1, 2, 3)] + [at_y(j) for j in NEAR] + [at_z(j) for j in NEAR] + [sib]
    for p in partners:
        pl.semaphore_signal(barrier, 1, device_id=p, device_id_type=MESH)
    own.wait()
    pl.semaphore_wait(barrier, len(partners))

    for j in FAR:
        push(rg.at[x, y], rg.at[x, y], gsend.at[0], gy.at[y], at_y(j))
    for i in (2, 1, 3):
        push(rg.at[x, y], rg.at[x, y], gsend.at[1], gx.at[x], at_x(i))
    to_sib = [
        push(wenc.at[:, pl.ds(pl.multiple_of((1 - c) * HALF, 128), HALF)], we.at[1],
             sib_send.at[0], sib_recv.at[0], sib),
        push(benc, bs, sib_send.at[1], sib_recv.at[1], sib),
    ]
    for hh in range(2):
        to_sib.append(
            push(wdec.at[:, pl.ds(pl.multiple_of((2 * (1 - c) + hh) * Q, 128), Q)], wds.at[hh],
                 sib_send.at[2 + hh], sib_recv.at[2 + hh], sib))

    def pass_on(n, carry):
        yy = (y + near_step(n)) % NY
        took(rg.at[x, yy], gsend.at[0], gy.at[yy]).wait_recv()
        for i in (2, 1, 3):
            push(rg.at[x, yy], rg.at[x, yy], gsend.at[1], gx.at[x], at_x(i))
        return carry

    lax.fori_loop(0, 7, pass_on, 0)

    for copy in dec_load:
        copy.wait()
    norm2 = jnp.zeros((LAT, 1), F32)
    for q in range(4):
        w = wd[q].astype(F32)
        norm2 = norm2 + jnp.sum(w * w, axis=1, keepdims=True)
    norm_col = jnp.sqrt(norm2 + epsilon)
    norm_row = jnp.transpose(jnp.broadcast_to(norm_col, (LAT, 128)))[0:1, :]

    enc_load.wait()
    for i in (1, 3, 2):
        xx = (x + i) % NX
        took(rg.at[xx], gsend.at[1], gx.at[xx]).wait_recv()
    for kk in range(2):
        even, odd = rg[2 * kk].astype(F32), rg[2 * kk + 1].astype(F32)
        both = jnp.concatenate([even, odd], axis=1).reshape(64, HALF)
        lhs[kk * 64:(kk + 1) * 64, :] = both.astype(BF16)
    to_sib[0].wait_recv()
    to_sib[1].wait_recv()
    rows = lhs[...]
    contract = (((1,), (1,)), ((), ()))
    for o in range(2):
        px[o] = lax.dot_general(rows, we[o], contract, preferred_element_type=F32)
    pre_copy = push(px, pr, pr_sem.at[0], pr_sem.at[1], sib)
    pre_copy.wait_recv()
    cc[0] = jnp.maximum(px[0] + pr[1] + benc[...], 0.0).astype(BF16)
    cc[1] = jnp.maximum(px[1] + pr[0] + bs[...], 0.0).astype(BF16)

    for hh in range(2):
        to_sib[2 + hh].wait_recv()

    def decode(hq):
        total = jnp.dot(cc[0], wd[2 * c + hq], preferred_element_type=F32)
        total = total + jnp.dot(cc[1], wds[hq], preferred_element_type=F32)
        part[hq] = total.astype(BF16).reshape(2, NY, 8, Q)

    decode(1 - h)

    def scatter_odd(n, carry):
        yy = (y + far_step(n)) % NY
        for kk in range(2):
            xx = 2 * kk + 1 - h
            slot = (xx - x + NX) % NX - 1
            push(part.at[1 - h, kk, yy], got.at[yy, slot], rsend.at[0], rx.at[yy], dev(xx, y, z, c))
        return carry

    lax.fori_loop(0, NY, scatter_odd, 0)
    decode(h)

    def scatter_even(n, carry):
        yy = (y + far_step(n)) % NY
        push(part.at[h, 1 - k, yy], got.at[yy, 1], rsend.at[0], rx.at[yy], at_x(2))
        return carry

    lax.fori_loop(0, NY, scatter_even, 0)

    codes_f32 = cc[0].astype(F32)
    sums_row = jnp.sum(codes_f32, axis=0, keepdims=True)
    sums_col = jnp.transpose(jnp.broadcast_to(sums_row, (128, LAT)))[:, 0:1]
    pbx[x] = jnp.broadcast_to(jnp.sum(sums_row * norm_row), (8, 128))
    for i in (1, 2, 3):
        push(pbx.at[x], pbx.at[x], pen_send.at[0], pen_recv.at[0], at_x(i))

    def piece_sum(yy):
        total = part[h, k, yy].astype(F32)
        for i in range(3):
            total = total + got[yy, i].astype(F32)
        return total

    def scatter_y(n, carry):
        step = far_step(n)
        yy = (y + step) % NY
        took(got.at[yy], rsend.at[0], rx.at[yy]).wait_recv()
        mid[yy] = piece_sum(yy).astype(BF16)
        push(mid.at[yy], ups.at[step - 1], rsend.at[1], ry.at[0], at_y(step))
        return carry

    lax.fori_loop(0, 7, scatter_y, 0)
    took(pbx.at[pl.ds(0, 3)], pen_send.at[0], pen_recv.at[0]).wait_recv()
    pbx_sum = pbx[0] + pbx[1] + pbx[2] + pbx[3]
    pby[y] = pbx_sum
    for j in FAR:
        push(pby.at[y], pby.at[y], pen_send.at[1], pen_recv.at[1], at_y(j))
    took(got.at[y], rsend.at[0], rx.at[y]).wait_recv()
    acc = piece_sum(y)
    took(ups, rsend.at[1], ry.at[0]).wait_recv()
    for j in range(7):
        acc = acc + ups[j].astype(F32)
    zb[z] = acc.astype(BF16)
    for j in FAR:
        push(zb.at[z], zb.at[z], rsend.at[2], rz.at[0], at_z(j))

    cols = pl.ds(pl.multiple_of(h * Q, 128), Q)
    rows8 = jnp.concatenate([rg[2 * k, y, :, cols].astype(F32), rg[2 * k + 1, y, :, cols].astype(F32)], axis=0)
    bias = bdec[pl.ds(2 * c + h, 1), :]
    took(zb.at[pl.ds(0, 7)], rsend.at[2], rz.at[0]).wait_recv()
    total = zb[0].astype(F32)
    for j in range(1, NZ):
        total = total + zb[j].astype(F32)
    piece = total + bias
    err[c, x, y] = (piece - rows8).astype(BF16)
    rc[c, h] = piece
    for j in FAR:
        push(err.at[c, x, y], err.at[c, x, y], esend.at[0], ey.at[y], at_y(j))
    for i in (2, 1, 3):
        push(err.at[c, x, y], err.at[c, x, y], esend.at[1], ex.at[x], at_x(i))
    beside = dev(x + 1 - 2 * h, y, z, c)
    push(rc.at[c, h], rc.at[c, h], rc_sem.at[0], rc_sem.at[1], beside)
    took(pby.at[pl.ds(0, 7)], pen_send.at[1], pen_recv.at[1]).wait_recv()
    pen = pby[0]
    for j in range(1, NY):
        pen = pen + pby[j]
    pbz[z] = pen
    for j in FAR:
        push(pbz.at[z], pbz.at[z], pen_send.at[2], pen_recv.at[2], at_z(j))

    def pass_err(n, carry):
        yy = (y + near_step(n)) % NY
        took(err.at[c, x, yy], esend.at[0], ey.at[yy]).wait_recv()
        for i in (2, 1, 3):
            push(err.at[c, x, yy], err.at[c, x, yy], esend.at[1], ex.at[x], at_x(i))
        return carry

    lax.fori_loop(0, 7, pass_err, 0)
    push(err.at[c, x], err.at[c, x], esend.at[2], es.at[x], sib)
    took(rc.at[c, h], rc_sem.at[0], rc_sem.at[1]).wait_recv()
    push(rc.at[c], rc.at[c], rc_sem.at[2], rc_sem.at[3], sib)
    took(pbz.at[pl.ds(0, 7)], pen_send.at[2], pen_recv.at[2]).wait_recv()
    pen = pbz[0]
    for j in range(1, NZ):
        pen = pen + pbz[j]
    pbc[c] = pen
    push(pbc.at[c], pbc.at[c], pen_send.at[3], pen_recv.at[3], sib)
    for i in (2, 1, 3):
        xx = (x + i) % NX
        took(err.at[c, xx], esend.at[1], ex.at[xx]).wait_recv()
        push(err.at[c, xx], err.at[c, xx], esend.at[2], es.at[xx], sib)

    codes = cc[0]
    ratio = sums_col / norm_col

    def quarter(co, hq, cg):
        q = 2 * co + hq
        e = jnp.concatenate([err[co, hq].reshape(64, Q), err[co, 2 + hq].reshape(64, Q)], axis=0)
        w = wd[q]
        grad = lax.dot_general(codes, e, (((0,), (0,)), ((), ())), preferred_element_type=F32)
        gws[q] = (grad + ratio * w.astype(F32)).astype(BF16)
        pltpu.make_async_copy(
            gws.at[q], gw_o.at[:, pl.ds(pl.multiple_of(q * Q, 128), Q)], out_sem.at[q]).start()
        cg = cg + lax.dot_general(e, w, contract, preferred_element_type=F32)
        ef = e.astype(F32)
        gb_o[pl.ds(q, 1), :] = jnp.sum(ef, axis=0, keepdims=True)
        return cg, ef

    cg = jnp.zeros((ROWS, LAT), F32)
    cg, _ = quarter(c, h, cg)
    cg, _ = quarter(c, 1 - h, cg)
    for xx in range(4):
        took(err.at[1 - c, xx], esend.at[2], es.at[xx]).wait_recv()
    cg, _ = quarter(1 - c, 0, cg)
    cg, _ = quarter(1 - c, 1, cg)

    for kk in range(2):
        for yy in range(NY):
            at = kk * 64 + yy * 8
            cg_o[16 * yy + 8 * kk:16 * yy + 8 * kk + 8, :] = cg[at:at + 8] + norm_row

    squares = jnp.zeros((8, Q), F32)
    for co in range(2):
        for xx in range(NX):
            e = err[co, xx].astype(F32)
            squares = squares + jnp.sum(e * e, axis=0)
    took(pbc.at[c], pen_send.at[3], pen_recv.at[3]).wait_recv()
    loss_o[...] = (0.5 * jnp.sum(squares) + (pbc[0] + pbc[1])) * SCALE

    took(rc.at[c], rc_sem.at[2], rc_sem.at[3]).wait_recv()
    for co in range(2):
        for hq in range(2):
            q = 2 * co + hq
            v = rc[co, hq]
            recon_o[:, q * Q:(q + 1) * Q] = jnp.where(h == 0, v[0:4], v[4:8])

    took(rg.at[0, pl.ds(0, 7)], gsend.at[0], gy.at[0]).wait_send()
    took(rg.at[pl.ds(0, 3)], gsend.at[1], gx.at[0]).wait_send()
    for copy in to_sib:
        copy.wait_send()
    pre_copy.wait_send()
    took(got, rsend.at[0], rx.at[0]).wait_send()
    took(ups, rsend.at[1], ry.at[0]).wait_send()
    took(zb.at[pl.ds(0, 7)], rsend.at[2], rz.at[0]).wait_send()
    took(err.at[0, 0, pl.ds(0, 7)], esend.at[0], ey.at[0]).wait_send()
    took(err.at[0, pl.ds(0, 3)], esend.at[1], ex.at[0]).wait_send()
    took(err.at[0], esend.at[2], es.at[0]).wait_send()
    took(rc.at[0, 0], rc_sem.at[0], rc_sem.at[1]).wait_send()
    took(rc.at[0], rc_sem.at[2], rc_sem.at[3]).wait_send()
    took(pbx.at[pl.ds(0, 3)], pen_send.at[0], pen_recv.at[0]).wait_send()
    took(pby.at[pl.ds(0, 7)], pen_send.at[1], pen_recv.at[1]).wait_send()
    took(pbz.at[pl.ds(0, 7)], pen_send.at[2], pen_recv.at[2]).wait_send()
    took(pbc.at[0], pen_send.at[3], pen_recv.at[3]).wait_send()
    for q in range(4):
        pltpu.make_async_copy(gws.at[q], gw_o.at[:, q * Q:(q + 1) * Q], out_sem.at[q]).wait()


def per_device(resid, w_enc, b_enc, w_dec, b_dec):
    anywhere = pl.BlockSpec(memory_space=pl.ANY)
    vmem = pl.BlockSpec(memory_space=pltpu.VMEM)
    dma = pltpu.SemaphoreType.DMA
    recon, grad_w_dec, code_grad, grad_b_dec, loss = pl.pallas_call(
        kernel,
        out_shape=(
            jax.ShapeDtypeStruct((4, D), F32),
            jax.ShapeDtypeStruct((LAT, D), BF16),
            jax.ShapeDtypeStruct((ROWS, LAT), F32),
            jax.ShapeDtypeStruct((4, Q), F32),
            jax.ShapeDtypeStruct((8, 128), F32),
        ),
        in_specs=[anywhere, anywhere, vmem, anywhere, vmem],
        out_specs=(vmem, anywhere, vmem, vmem, vmem),
        scratch_shapes=[
            pltpu.VMEM((NX, NY, 4, HALF), BF16),
            pltpu.VMEM((2, LAT, HALF), BF16),
            pltpu.VMEM((4, LAT, Q), BF16),
            pltpu.VMEM((2, LAT, Q), BF16),
            pltpu.VMEM((1, LAT), F32),
            pltpu.VMEM((ROWS, HALF), BF16),
            pltpu.VMEM((2, ROWS, LAT), F32),
            pltpu.VMEM((2, ROWS, LAT), F32),
            pltpu.VMEM((2, ROWS, LAT), BF16),
            pltpu.VMEM((2, 2, NY, 8, Q), BF16),
            pltpu.VMEM((NY, 3, 8, Q), BF16),
            pltpu.VMEM((NY, 8, Q), BF16),
            pltpu.VMEM((7, 8, Q), BF16),
            pltpu.VMEM((NZ, 8, Q), BF16),
            pltpu.VMEM((2, NX, NY, 8, Q), BF16),
            pltpu.VMEM((2, 2, 8, Q), F32),
            pltpu.VMEM((4, LAT, Q), BF16),
            pltpu.VMEM((NX, 8, 128), F32),
            pltpu.VMEM((NY, 8, 128), F32),
            pltpu.VMEM((NZ, 8, 128), F32),
            pltpu.VMEM((2, 8, 128), F32),
            dma((6,)),
            dma((NY,)),
            dma((NX,)),
            dma((2,)),
            dma((4,)),
            dma((4,)),
            dma((2,)),
            dma((NY,)),
            dma((1,)),
            dma((1,)),
            dma((3,)),
            dma((NY,)),
            dma((NX,)),
            dma((NX,)),
            dma((3,)),
            dma((4,)),
            dma((4,)),
            dma((4,)),
            dma((4,)),
        ],
        compiler_params=pltpu.CompilerParams(
            collective_id=0, has_side_effects=True, vmem_limit_bytes=48 << 20
        ),
        cost_estimate=pl.CostEstimate(flops=900_000_000, bytes_accessed=6_000_000, transcendentals=0),
    )(resid, w_enc, b_enc.reshape(1, LAT), w_dec, b_dec.reshape(4, Q))
    return recon, grad_w_dec, code_grad, grad_b_dec.reshape(D), loss[0, 0]


def solution(mesh):
    in_specs = (
        P("tensor", None),
        P(("section", "tensor"), None),
        P(("section", "tensor")),
        P(("section", "tensor"), None),
        P(),
    )
    out_specs = (
        P("tensor", None),
        P(("section", "tensor"), None),
        P(None, ("section", "tensor")),
        P(),
        P(),
    )
    return jax.shard_map(
        per_device, mesh=mesh, in_specs=in_specs, out_specs=out_specs, check_vma=False
    )
```

time: 361 us -> 68.1 us (0.19)
  waiting for transfers between devices: 179 us -> 0 us
  blocking collectives: 154 us -> 0 us
  Pallas kernels: 0 us -> 58.5 us
  between operations: 16.4 us -> 0.65 us
  local copies, waits for them, and re-layouts: 0.87 us -> 8.64 us
  matrix products: 6.08 us -> 0 us
  other arithmetic: 4.75 us -> 0 us
    psum x1 -> x0, waiting for transfers between devices: 179 us -> none  [per_device(): summed = lax.psum(partial_value, ('section', 'tensor'))]
    psum x1 -> x0, blocking collectives: 114 us -> none  [per_device(): penalty = lax.psum(jnp.sum(codes_f32 * dec_norm), ('section', 'tensor'))]
    pallas_call x0 -> x1, Pallas kernels: none -> 58.5 us  [per_device(): pl.pallas_call(kernel, out_shape=(jax.ShapeDtypeStruct((4, D), F32), jax....]
    all_gather x1 -> x0, blocking collectives: 40.3 us -> none  [per_device(): stream = lax.all_gather(resid, 'tensor', axis=0, tiled=True)]
    unnamed x11, local copies, waits for them, and re-layouts: 0.24 us -> 6.78 us
    dot_general x4 -> x0, matrix products: 6.08 us -> none  [the longest x1 1.95 us: per_device(): lax.dot_general(codes, err_half, (((0,), (0,)), ((), ())), preferred_elem...]
    reduce_sum x2 -> x0, other arithmetic: 4.74 us -> none  [the longest x1 2.81 us: per_device(): squares = jnp.sum(errors * errors)]
  transfers between devices with their start and end apart: 1 -> 0, of which waited for: 1 -> 0; matrix products, arithmetic and copies ran while one was open for 0% -> 0% of each run, Pallas kernels for 0% -> 0%
where the time goes in v1:
time: 68.1 us; the launch traced here: 67.8 us
  Pallas kernels  58.5 us (86%)
  local copies, waits for them, and re-layouts  8.64 us (13%)
    pallas_call x1, Pallas kernels, per_device(): pl.pallas_call(kernel, out_shape=(jax.ShapeDtypeStruct((4, D), F32), jax....  58.5 us
    unnamed x11, local copies, waits for them, and re-layouts  6.78 us

profile of v1, /device:TPU:1, one launch (start us, length us, event | category | flops | bytes accessed | tf_op | source)
XLA Modules:
  0.0 67.8 jit_solution(5267093581335750267)
XLA Ops:
  0.6 0.7 %reshape.20.bdec = f32[4,896]{1,0:T(4,128)S(1)} reshape(f32[3584]{0:T(1024)} %param.9) | data formatting | bytes 28672 | tf_op jit(solution)/shard_map/reshape | solution.py:371
  1.4 0.0 copy-start
  1.4 1.4 %copy-done = bf16[224,3584]{1,0:T(8,128)(2,1)S(1)} copy-done((bf16[224,3584]{1,0:T(8,128)(2,1)S(1)}, bf16[224,3584]{1,0:T(8,128)(2,1)}, u32[]{:S(2)}) %copy-start) | copy-done | bytes 1605656
  2.8 0.0 copy-start.1
  2.8 1.4 %copy-done.1 = bf16[224,3584]{1,0:T(8,128)(2,1)S(1)} copy-done((bf16[224,3584]{1,0:T(8,128)(2,1)S(1)}, bf16[224,3584]{1,0:T(8,128)(2,1)}, u32[]{:S(2)}) %copy-start.1) | copy-done | bytes 1605656
  4.2 0.0 copy-start.2
  4.2 0.7 %copy-done.2 = bf16[4,3584]{1,0:T(4,128)(2,1)S(1)} copy-done((bf16[4,3584]{1,0:T(4,128)(2,1)S(1)}, bf16[4,3584]{1,0:T(4,128)(2,1)}, u32[]{:S(2)}) %copy-start.2) | copy-done | bytes 28696
  4.9 0.0 copy-start.3
  4.9 0.7 copy-done.3
  5.6 58.5 %shard_map.92 = (f32[4,3584]{1,0:T(4,128)S(1)}, bf16[224,3584]{1,0:T(8,128)(2,1)S(1)}, f32[128,224]{1,0:T(8,128)S(1)}, f32[4,896]{1,0:T(4,128)S(1)}, f32[8,128]{1,0:T(8,128)S(1)}) custom-call(bf16[4,3584]{1,0:T(4,128)(2,1)S(1)} %copy-done.2, bf16[224,3584]{1,0:T(8,128)(2,1)S(1)} %copy-done, f32[1,224]{1,0:T(1,128)S(1)} %bitcast.2, ...), custom_call_target="tpu_custom_call" | custom-call | flops 900000000 | bytes 6000000 | tf_op jit(solution)/shard_map/pallas_call | solution.py:314
  64.2 0.5 slice.3
  64.7 0.6 reshape.21
  65.3 0.7 %copy.10 = f32[128,224]{0,1:T(8,128)} copy(f32[128,224]{1,0:T(8,128)S(1)} %get-tuple-element.17) | data formatting | bytes 229376
  66.0 0.6 copy.13
  66.7 1.2 %copy.14 = bf16[224,3584]{1,0:T(8,128)(2,1)} copy(bf16[224,3584]{1,0:T(8,128)(2,1)S(1)} %get-tuple-element.26) | data formatting | bytes 3211264
Async XLA Ops:
  1.4 1.4 %copy-start = (bf16[224,3584]{1,0:T(8,128)(2,1)S(1)}, bf16[224,3584]{1,0:T(8,128)(2,1)}, u32[]{:S(2)}) copy-start(bf16[224,3584]{1,0:T(8,128)(2,1)} %wenc.1) | copy-start | bytes 4816900
  2.8 1.4 %copy-start.1 = (bf16[224,3584]{1,0:T(8,128)(2,1)S(1)}, bf16[224,3584]{1,0:T(8,128)(2,1)}, u32[]{:S(2)}) copy-start(bf16[224,3584]{1,0:T(8,128)(2,1)} %wdec.1) | copy-start | bytes 4816900
  4.2 0.7 %copy-start.2 = (bf16[4,3584]{1,0:T(4,128)(2,1)S(1)}, bf16[4,3584]{1,0:T(4,128)(2,1)}, u32[]{:S(2)}) copy-start(bf16[4,3584]{1,0:T(4,128)(2,1)} %resid.1) | copy-start | bytes 86020
  4.9 0.7 %copy-start.3 = (f32[224]{0:T(256)S(1)}, f32[224]{0:T(256)}, u32[]{:S(2)}) copy-start(f32[224]{0:T(256)} %param.7) | copy-start | bytes 2692

commit v2 on v1

--- a/solution.py
+++ b/solution.py
@@ -30,10 +30,10 @@
 def kernel(
     resid, wenc, benc, wdec, bdec,
     recon_o, gw_o, cg_o, gb_o, loss_o,
-    rg, we, wd, wds, bs, lhs, px, pr, cc, part, got, mid, ups, zb, err, rc, gws,
+    rg, we, wd, wds, bo, bs, bd, lhs, px, pr, cc, part, got, mid, ups, zb, err, rc,
     pbx, pby, pbz, pbc,
     load_sem, gy, gx, gsend, sib_send, sib_recv, pr_sem,
-    rx, ry, rz, rsend, ey, ex, es, esend, rc_sem, pen_recv, pen_send, out_sem,
+    rx, ry, rz, rsend, ey, ex, es, esend, rc_sem, pen_recv, pen_send,
 ):
     section, tensor = lax.axis_index("section"), lax.axis_index("tensor")
     z, c = section // 2, section % 2
@@ -61,6 +61,8 @@
 
     def took(ref, ssem, rsem):
         return pltpu.make_async_remote_copy(ref, ref, ssem, rsem, device_id=sib, device_id_type=MESH)
+
+    sent = []
 
     own = pltpu.make_async_copy(
         resid.at[:, pl.ds(pl.multiple_of(c * HALF, 128), HALF)], rg.at[x, y], load_sem.at[0])
@@ -72,6 +74,12 @@
         pltpu.make_async_copy(wdec.at[:, q * Q:(q + 1) * Q], wd.at[q], load_sem.at[2 + q]) for q in range(4)
     ]
     for copy in dec_load:
+        copy.start()
+    bias_load = [
+        pltpu.make_async_copy(benc, bo, load_sem.at[6]),
+        pltpu.make_async_copy(bdec, bd, load_sem.at[7]),
+    ]
+    for copy in bias_load:
         copy.start()
 
     barrier = pltpu.get_barrier_semaphore()
@@ -103,6 +111,9 @@
         return carry
 
     lax.fori_loop(0, 7, pass_on, 0)
+    sent.append(took(rg.at[0, pl.ds(0, 7)], gsend.at[0], gy.at[0]))
+    sent.append(took(rg.at[pl.ds(0, 3)], gsend.at[1], gx.at[0]))
+    sent.extend(to_sib)
 
     for copy in dec_load:
         copy.wait()
@@ -119,17 +130,19 @@
         took(rg.at[xx], gsend.at[1], gx.at[xx]).wait_recv()
     for kk in range(2):
         even, odd = rg[2 * kk].astype(F32), rg[2 * kk + 1].astype(F32)
-        both = jnp.concatenate([even, odd], axis=1).reshape(64, HALF)
-        lhs[kk * 64:(kk + 1) * 64, :] = both.astype(BF16)
+        lhs[:, kk] = jnp.concatenate([even, odd], axis=1).astype(BF16)
     to_sib[0].wait_recv()
     to_sib[1].wait_recv()
-    rows = lhs[...]
+    rows = lhs[...].reshape(ROWS, HALF)
+    for copy in bias_load:
+        copy.wait()
     contract = (((1,), (1,)), ((), ()))
     for o in range(2):
         px[o] = lax.dot_general(rows, we[o], contract, preferred_element_type=F32)
     pre_copy = push(px, pr, pr_sem.at[0], pr_sem.at[1], sib)
+    sent.append(pre_copy)
     pre_copy.wait_recv()
-    cc[0] = jnp.maximum(px[0] + pr[1] + benc[...], 0.0).astype(BF16)
+    cc[0] = jnp.maximum(px[0] + pr[1] + bo[...], 0.0).astype(BF16)
     cc[1] = jnp.maximum(px[1] + pr[0] + bs[...], 0.0).astype(BF16)
 
     for hh in range(2):
@@ -138,7 +151,7 @@
     def decode(hq):
         total = jnp.dot(cc[0], wd[2 * c + hq], preferred_element_type=F32)
         total = total + jnp.dot(cc[1], wds[hq], preferred_element_type=F32)
-        part[hq] = total.astype(BF16).reshape(2, NY, 8, Q)
+        part[hq] = total.astype(BF16).reshape(NY, 2, 8, Q)
 
     decode(1 - h)
 
@@ -147,7 +160,7 @@
         for kk in range(2):
             xx = 2 * kk + 1 - h
             slot = (xx - x + NX) % NX - 1
-            push(part.at[1 - h, kk, yy], got.at[yy, slot], rsend.at[0], rx.at[yy], dev(xx, y, z, c))
+            push(part.at[1 - h, yy, kk], got.at[yy, slot], rsend.at[0], rx.at[yy], dev(xx, y, z, c))
         return carry
 
     lax.fori_loop(0, NY, scatter_odd, 0)
@@ -155,10 +168,11 @@
 
     def scatter_even(n, carry):
         yy = (y + far_step(n)) % NY
-        push(part.at[h, 1 - k, yy], got.at[yy, 1], rsend.at[0], rx.at[yy], at_x(2))
+        push(part.at[h, yy, 1 - k], got.at[yy, 1], rsend.at[0], rx.at[yy], at_x(2))
         return carry
 
     lax.fori_loop(0, NY, scatter_even, 0)
+    sent.append(took(got, rsend.at[0], rx.at[0]))
 
     codes_f32 = cc[0].astype(F32)
     sums_row = jnp.sum(codes_f32, axis=0, keepdims=True)
@@ -166,9 +180,10 @@
     pbx[x] = jnp.broadcast_to(jnp.sum(sums_row * norm_row), (8, 128))
     for i in (1, 2, 3):
         push(pbx.at[x], pbx.at[x], pen_send.at[0], pen_recv.at[0], at_x(i))
+    sent.append(took(pbx.at[pl.ds(0, 3)], pen_send.at[0], pen_recv.at[0]))
 
     def piece_sum(yy):
-        total = part[h, k, yy].astype(F32)
+        total = part[h, yy, k].astype(F32)
         for i in range(3):
             total = total + got[yy, i].astype(F32)
         return total
@@ -182,11 +197,13 @@
         return carry
 
     lax.fori_loop(0, 7, scatter_y, 0)
+    sent.append(took(ups, rsend.at[1], ry.at[0]))
     took(pbx.at[pl.ds(0, 3)], pen_send.at[0], pen_recv.at[0]).wait_recv()
     pbx_sum = pbx[0] + pbx[1] + pbx[2] + pbx[3]
     pby[y] = pbx_sum
     for j in FAR:
         push(pby.at[y], pby.at[y], pen_send.at[1], pen_recv.at[1], at_y(j))
+    sent.append(took(pby.at[pl.ds(0, 7)], pen_send.at[1], pen_recv.at[1]))
     took(got.at[y], rsend.at[0], rx.at[y]).wait_recv()
     acc = piece_sum(y)
     took(ups, rsend.at[1], ry.at[0]).wait_recv()
@@ -195,10 +212,12 @@
     zb[z] = acc.astype(BF16)
     for j in FAR:
         push(zb.at[z], zb.at[z], rsend.at[2], rz.at[0], at_z(j))
+    sent.append(took(zb.at[pl.ds(0, 7)], rsend.at[2], rz.at[0]))
 
     cols = pl.ds(pl.multiple_of(h * Q, 128), Q)
     rows8 = jnp.concatenate([rg[2 * k, y, :, cols].astype(F32), rg[2 * k + 1, y, :, cols].astype(F32)], axis=0)
-    bias = bdec[pl.ds(2 * c + h, 1), :]
+    first = (2 * c + h) * 7
+    bias = jnp.concatenate([bd[pl.ds(first + i, 1), :] for i in range(7)], axis=1)
     took(zb.at[pl.ds(0, 7)], rsend.at[2], rz.at[0]).wait_recv()
     total = zb[0].astype(F32)
     for j in range(1, NZ):
@@ -212,6 +231,7 @@
         push(err.at[c, x, y], err.at[c, x, y], esend.at[1], ex.at[x], at_x(i))
     beside = dev(x + 1 - 2 * h, y, z, c)
     push(rc.at[c, h], rc.at[c, h], rc_sem.at[0], rc_sem.at[1], beside)
+    sent.append(took(rc.at[0, 0], rc_sem.at[0], rc_sem.at[1]))
     took(pby.at[pl.ds(0, 7)], pen_send.at[1], pen_recv.at[1]).wait_recv()
     pen = pby[0]
     for j in range(1, NY):
@@ -219,6 +239,7 @@
     pbz[z] = pen
     for j in FAR:
         push(pbz.at[z], pbz.at[z], pen_send.at[2], pen_recv.at[2], at_z(j))
+    sent.append(took(pbz.at[pl.ds(0, 7)], pen_send.at[2], pen_recv.at[2]))
 
     def pass_err(n, carry):
         yy = (y + near_step(n)) % NY
@@ -228,48 +249,47 @@
         return carry
 
     lax.fori_loop(0, 7, pass_err, 0)
+    sent.append(took(err.at[0, 0, pl.ds(0, 7)], esend.at[0], ey.at[0]))
+    sent.append(took(err.at[0, pl.ds(0, 3)], esend.at[1], ex.at[0]))
     push(err.at[c, x], err.at[c, x], esend.at[2], es.at[x], sib)
     took(rc.at[c, h], rc_sem.at[0], rc_sem.at[1]).wait_recv()
     push(rc.at[c], rc.at[c], rc_sem.at[2], rc_sem.at[3], sib)
+    sent.append(took(rc.at[0], rc_sem.at[2], rc_sem.at[3]))
     took(pbz.at[pl.ds(0, 7)], pen_send.at[2], pen_recv.at[2]).wait_recv()
     pen = pbz[0]
     for j in range(1, NZ):
         pen = pen + pbz[j]
     pbc[c] = pen
     push(pbc.at[c], pbc.at[c], pen_send.at[3], pen_recv.at[3], sib)
+    sent.append(took(pbc.at[0], pen_send.at[3], pen_recv.at[3]))
     for i in (2, 1, 3):
         xx = (x + i) % NX
         took(err.at[c, xx], esend.at[1], ex.at[xx]).wait_recv()
         push(err.at[c, xx], err.at[c, xx], esend.at[2], es.at[xx], sib)
+    sent.append(took(err.at[0], esend.at[2], es.at[0]))
 
     codes = cc[0]
     ratio = sums_col / norm_col
 
     def quarter(co, hq, cg):
         q = 2 * co + hq
-        e = jnp.concatenate([err[co, hq].reshape(64, Q), err[co, 2 + hq].reshape(64, Q)], axis=0)
+        e = jnp.stack([err[co, hq], err[co, 2 + hq]], axis=1).reshape(ROWS, Q)
         w = wd[q]
         grad = lax.dot_general(codes, e, (((0,), (0,)), ((), ())), preferred_element_type=F32)
-        gws[q] = (grad + ratio * w.astype(F32)).astype(BF16)
-        pltpu.make_async_copy(
-            gws.at[q], gw_o.at[:, pl.ds(pl.multiple_of(q * Q, 128), Q)], out_sem.at[q]).start()
-        cg = cg + lax.dot_general(e, w, contract, preferred_element_type=F32)
-        ef = e.astype(F32)
-        gb_o[pl.ds(q, 1), :] = jnp.sum(ef, axis=0, keepdims=True)
-        return cg, ef
-
-    cg = jnp.zeros((ROWS, LAT), F32)
-    cg, _ = quarter(c, h, cg)
-    cg, _ = quarter(c, 1 - h, cg)
+        gw_o[q] = (grad + ratio * w.astype(F32)).astype(BF16)
+        sums = jnp.sum(e.astype(F32), axis=0, keepdims=True)
+        for i in range(7):
+            gb_o[pl.ds(7 * q + i, 1), :] = sums[:, i * 128:(i + 1) * 128]
+        return cg + lax.dot_general(w, e, contract, preferred_element_type=F32)
+
+    cg = jnp.zeros((LAT, ROWS), F32)
+    cg = quarter(c, h, cg)
+    cg = quarter(c, 1 - h, cg)
     for xx in range(4):
         took(err.at[1 - c, xx], esend.at[2], es.at[xx]).wait_recv()
-    cg, _ = quarter(1 - c, 0, cg)
-    cg, _ = quarter(1 - c, 1, cg)
-
-    for kk in range(2):
-        for yy in range(NY):
-            at = kk * 64 + yy * 8
-            cg_o[16 * yy + 8 * kk:16 * yy + 8 * kk + 8, :] = cg[at:at + 8] + norm_row
+    cg = quarter(1 - c, 0, cg)
+    cg = quarter(1 - c, 1, cg)
+    cg_o[...] = cg + norm_col
 
     squares = jnp.zeros((8, Q), F32)
     for co in range(2):
@@ -286,65 +306,63 @@
             v = rc[co, hq]
             recon_o[:, q * Q:(q + 1) * Q] = jnp.where(h == 0, v[0:4], v[4:8])
 
-    took(rg.at[0, pl.ds(0, 7)], gsend.at[0], gy.at[0]).wait_send()
-    took(rg.at[pl.ds(0, 3)], gsend.at[1], gx.at[0]).wait_send()
-    for copy in to_sib:
+    for copy in sent:
         copy.wait_send()
-    pre_copy.wait_send()
-    took(got, rsend.at[0], rx.at[0]).wait_send()
-    took(ups, rsend.at[1], ry.at[0]).wait_send()
-    took(zb.at[pl.ds(0, 7)], rsend.at[2], rz.at[0]).wait_send()
-    took(err.at[0, 0, pl.ds(0, 7)], esend.at[0], ey.at[0]).wait_send()
-    took(err.at[0, pl.ds(0, 3)], esend.at[1], ex.at[0]).wait_send()
-    took(err.at[0], esend.at[2], es.at[0]).wait_send()
-    took(rc.at[0, 0], rc_sem.at[0], rc_sem.at[1]).wait_send()
-    took(rc.at[0], rc_sem.at[2], rc_sem.at[3]).wait_send()
-    took(pbx.at[pl.ds(0, 3)], pen_send.at[0], pen_recv.at[0]).wait_send()
-    took(pby.at[pl.ds(0, 7)], pen_send.at[1], pen_recv.at[1]).wait_send()
-    took(pbz.at[pl.ds(0, 7)], pen_send.at[2], pen_recv.at[2]).wait_send()
-    took(pbc.at[0], pen_send.at[3], pen_recv.at[3]).wait_send()
-    for q in range(4):
-        pltpu.make_async_copy(gws.at[q], gw_o.at[:, q * Q:(q + 1) * Q], out_sem.at[q]).wait()
+
+
+def write_out(recon, grad, code_grad, bias_grad, loss, recon_o, grad_o, code_grad_o, bias_grad_o, loss_o, sem):
+    copies = [pltpu.make_async_copy(grad.at[q], grad_o.at[:, q * Q:(q + 1) * Q], sem.at[q]) for q in range(4)]
+    copies += [
+        pltpu.make_async_copy(recon, recon_o, sem.at[4]),
+        pltpu.make_async_copy(code_grad, code_grad_o, sem.at[5]),
+        pltpu.make_async_copy(bias_grad, bias_grad_o, sem.at[6]),
+    ]
+    for copy in copies:
+        copy.start()
+    loss_o[...] = loss[0:1, 0:1]
+    for copy in copies:
+        copy.wait()
 
 
 def per_device(resid, w_enc, b_enc, w_dec, b_dec):
-    anywhere = pl.BlockSpec(memory_space=pl.ANY)
+    hbm = pl.BlockSpec(memory_space=pltpu.HBM)
     vmem = pl.BlockSpec(memory_space=pltpu.VMEM)
     dma = pltpu.SemaphoreType.DMA
-    recon, grad_w_dec, code_grad, grad_b_dec, loss = pl.pallas_call(
+    made = pl.pallas_call(
         kernel,
         out_shape=(
             jax.ShapeDtypeStruct((4, D), F32),
-            jax.ShapeDtypeStruct((LAT, D), BF16),
-            jax.ShapeDtypeStruct((ROWS, LAT), F32),
-            jax.ShapeDtypeStruct((4, Q), F32),
+            jax.ShapeDtypeStruct((4, LAT, Q), BF16),
+            jax.ShapeDtypeStruct((LAT, ROWS), F32),
+            jax.ShapeDtypeStruct((28, 128), F32),
             jax.ShapeDtypeStruct((8, 128), F32),
         ),
-        in_specs=[anywhere, anywhere, vmem, anywhere, vmem],
-        out_specs=(vmem, anywhere, vmem, vmem, vmem),
+        in_specs=[hbm] * 5,
+        out_specs=(vmem,) * 5,
         scratch_shapes=[
             pltpu.VMEM((NX, NY, 4, HALF), BF16),
             pltpu.VMEM((2, LAT, HALF), BF16),
             pltpu.VMEM((4, LAT, Q), BF16),
             pltpu.VMEM((2, LAT, Q), BF16),
             pltpu.VMEM((1, LAT), F32),
-            pltpu.VMEM((ROWS, HALF), BF16),
+            pltpu.VMEM((1, LAT), F32),
+            pltpu.VMEM((28, 128), F32),
+            pltpu.VMEM((NY, 2, 8, HALF), BF16),
             pltpu.VMEM((2, ROWS, LAT), F32),
             pltpu.VMEM((2, ROWS, LAT), F32),
             pltpu.VMEM((2, ROWS, LAT), BF16),
-            pltpu.VMEM((2, 2, NY, 8, Q), BF16),
+            pltpu.VMEM((2, NY, 2, 8, Q), BF16),
             pltpu.VMEM((NY, 3, 8, Q), BF16),
             pltpu.VMEM((NY, 8, Q), BF16),
             pltpu.VMEM((7, 8, Q), BF16),
             pltpu.VMEM((NZ, 8, Q), BF16),
             pltpu.VMEM((2, NX, NY, 8, Q), BF16),
             pltpu.VMEM((2, 2, 8, Q), F32),
-            pltpu.VMEM((4, LAT, Q), BF16),
             pltpu.VMEM((NX, 8, 128), F32),
             pltpu.VMEM((NY, 8, 128), F32),
             pltpu.VMEM((NZ, 8, 128), F32),
             pltpu.VMEM((2, 8, 128), F32),
-            dma((6,)),
+            dma((8,)),
             dma((NY,)),
             dma((NX,)),
             dma((2,)),
@@ -362,14 +380,27 @@
             dma((4,)),
             dma((4,)),
             dma((4,)),
-            dma((4,)),
         ],
         compiler_params=pltpu.CompilerParams(
             collective_id=0, has_side_effects=True, vmem_limit_bytes=48 << 20
         ),
         cost_estimate=pl.CostEstimate(flops=900_000_000, bytes_accessed=6_000_000, transcendentals=0),
-    )(resid, w_enc, b_enc.reshape(1, LAT), w_dec, b_dec.reshape(4, Q))
-    return recon, grad_w_dec, code_grad, grad_b_dec.reshape(D), loss[0, 0]
+    )(*[pltpu.with_memory_space_constraint(v, pltpu.HBM) for v in (resid, w_enc, b_enc.reshape(1, LAT), w_dec, b_dec.reshape(28, 128))])
+    recon, grad_w_dec, code_grad, grad_b_dec, loss = pl.pallas_call(
+        write_out,
+        out_shape=(
+            jax.ShapeDtypeStruct((4, D), F32),
+            jax.ShapeDtypeStruct((LAT, D), BF16),
+            jax.ShapeDtypeStruct((LAT, ROWS), F32),
+            jax.ShapeDtypeStruct((28, 128), F32),
+            jax.ShapeDtypeStruct((1, 1), F32),
+        ),
+        in_specs=[vmem] * 5,
+        out_specs=(hbm,) * 4 + (vmem,),
+        scratch_shapes=[dma((7,))],
+        compiler_params=pltpu.CompilerParams(vmem_limit_bytes=1 << 20),
+    )(*made)
+    return recon, grad_w_dec, code_grad.T, grad_b_dec.reshape(D), loss.reshape(())
 
 
 def solution(mesh):

time: 68.1 us -> 60.4 us (0.89)
  local copies, waits for them, and re-layouts: 8.64 us -> 0 us
  Pallas kernels: 58.5 us -> 59.5 us
    unnamed x11 -> x0, local copies, waits for them, and re-layouts: 6.78 us -> none
    pallas_call x0 -> x1, Pallas kernels: none -> 1.77 us  [per_device(): pl.pallas_call(write_out, out_shape=(jax.ShapeDtypeStruct((4, D), F32), j...]
    reshape x2 -> x0, local copies, waits for them, and re-layouts: 1.34 us -> none  [the longest x1 0.73 us: per_device(): b_dec.reshape(4, Q)]
    pallas_call x1, Pallas kernels: 58.5 us -> 57.8 us  [per_device(): pl.pallas_call(kernel, out_shape=(jax.ShapeDtypeStruct((4, D), F32), jax....]
where the time goes in v2:
time: 60.4 us; the launch traced here: 60.2 us
  Pallas kernels  59.5 us (99%)
  between operations  0.64 us (1%)
    pallas_call x1, Pallas kernels, per_device(): pl.pallas_call(kernel, out_shape=(jax.ShapeDtypeStruct((4, D), F32), jax....  57.8 us
    pallas_call x1, Pallas kernels, per_device(): pl.pallas_call(write_out, out_shape=(jax.ShapeDtypeStruct((4, D), F32), j...  1.77 us

profile of v2, /device:TPU:1, one launch (start us, length us, event | category | flops | bytes accessed | tf_op | source)
XLA Modules:
  0.0 60.2 jit_solution(16878892573988395585)
XLA Ops:
  0.6 57.8 %shard_map.92 = (f32[4,3584]{1,0:T(4,128)S(1)}, bf16[4,224,896]{2,1,0:T(8,128)(2,1)S(1)}, f32[224,128]{1,0:T(8,128)S(1)}, f32[28,128]{1,0:T(8,128)S(1)}, f32[8,128]{1,0:T(8,128)S(1)}) custom-call(bf16[4,3584]{1,0:T(4,128)(2,1)} %resid.1, bf16[224,3584]{1,0:T(8,128)(2,1)} %wenc.1, f32[1,224]{1,0:T(1,128)} %bitcast.8, bf16[224,3584]{1,0:T(8,128)(2,1)} %wdec.1, ...), custom_call_target="tpu_custom_call" | custom-call | flops 900000000 | bytes 6000000 | tf_op jit(solution)/shard_map/pallas_call | solution.py:331
  58.4 1.8 %shard_map.93 = (f32[4,3584]{1,0:T(4,128)}, bf16[224,3584]{1,0:T(8,128)(2,1)}, f32[224,128]{1,0:T(8,128)}, f32[28,128]{1,0:T(8,128)}, f32[1,1]{1,0:T(1,128)}) custom-call(f32[4,3584]{1,0:T(4,128)S(1)} %get-tuple-element.15.recon, bf16[4,224,896]{2,1,0:T(8,128)(2,1)S(1)} %get-tuple-element.16.grad, f32[224,128]{1,0:T(8,128)S(1)} %get-tuple-element.17.code_grad, ...), custom_call_target="tpu_custom_call" | custom-call | tf_op jit(solution)/shard_map/pallas_call | solution.py:389

commit v3 on v2

--- a/solution.py
+++ b/solution.py
@@ -89,10 +89,18 @@
     own.wait()
     pl.semaphore_wait(barrier, len(partners))
 
-    for j in FAR:
+    for j in NEAR:
         push(rg.at[x, y], rg.at[x, y], gsend.at[0], gy.at[y], at_y(j))
     for i in (2, 1, 3):
         push(rg.at[x, y], rg.at[x, y], gsend.at[1], gx.at[x], at_x(i))
+    def pass_on(n, carry):
+        yy = (y + near_step(n)) % NY
+        took(rg.at[x, yy], gsend.at[0], gy.at[yy]).wait_recv()
+        for i in (2, 1, 3):
+            push(rg.at[x, yy], rg.at[x, yy], gsend.at[1], gx.at[x], at_x(i))
+        return carry
+
+    lax.fori_loop(0, 7, pass_on, 0)
     to_sib = [
         push(wenc.at[:, pl.ds(pl.multiple_of((1 - c) * HALF, 128), HALF)], we.at[1],
              sib_send.at[0], sib_recv.at[0], sib),
@@ -102,15 +110,6 @@
         to_sib.append(
             push(wdec.at[:, pl.ds(pl.multiple_of((2 * (1 - c) + hh) * Q, 128), Q)], wds.at[hh],
                  sib_send.at[2 + hh], sib_recv.at[2 + hh], sib))
-
-    def pass_on(n, carry):
-        yy = (y + near_step(n)) % NY
-        took(rg.at[x, yy], gsend.at[0], gy.at[yy]).wait_recv()
-        for i in (2, 1, 3):
-            push(rg.at[x, yy], rg.at[x, yy], gsend.at[1], gx.at[x], at_x(i))
-        return carry
-
-    lax.fori_loop(0, 7, pass_on, 0)
     sent.append(took(rg.at[0, pl.ds(0, 7)], gsend.at[0], gy.at[0]))
     sent.append(took(rg.at[pl.ds(0, 3)], gsend.at[1], gx.at[0]))
     sent.extend(to_sib)
@@ -225,7 +224,7 @@
     piece = total + bias
     err[c, x, y] = (piece - rows8).astype(BF16)
     rc[c, h] = piece
-    for j in FAR:
+    for j in NEAR:
         push(err.at[c, x, y], err.at[c, x, y], esend.at[0], ey.at[y], at_y(j))
     for i in (2, 1, 3):
         push(err.at[c, x, y], err.at[c, x, y], esend.at[1], ex.at[x], at_x(i))

time: 60.4 us -> 57.8 us (0.957)
  Pallas kernels: 59.5 us -> 57 us
    pallas_call x1, Pallas kernels: 57.8 us -> 55.2 us  [per_device(): pl.pallas_call(kernel, out_shape=(jax.ShapeDtypeStruct((4, D), F32), jax....]
where the time goes in v3:
time: 57.8 us; the launch traced here: 57.7 us
  Pallas kernels  57 us (99%)
  between operations  0.64 us (1%)
    pallas_call x1, Pallas kernels, per_device(): pl.pallas_call(kernel, out_shape=(jax.ShapeDtypeStruct((4, D), F32), jax....  55.2 us
    pallas_call x1, Pallas kernels, per_device(): pl.pallas_call(write_out, out_shape=(jax.ShapeDtypeStruct((4, D), F32), j...  1.77 us

profile of v3, /device:TPU:1, one launch (start us, length us, event | category | flops | bytes accessed | tf_op | source)
XLA Modules:
  0.0 57.7 jit_solution(7075383047273628191)
XLA Ops:
  0.6 55.2 %shard_map.92 = (f32[4,3584]{1,0:T(4,128)S(1)}, bf16[4,224,896]{2,1,0:T(8,128)(2,1)S(1)}, f32[224,128]{1,0:T(8,128)S(1)}, f32[28,128]{1,0:T(8,128)S(1)}, f32[8,128]{1,0:T(8,128)S(1)}) custom-call(bf16[4,3584]{1,0:T(4,128)(2,1)} %resid.1, bf16[224,3584]{1,0:T(8,128)(2,1)} %wenc.1, f32[1,224]{1,0:T(1,128)} %bitcast.8, bf16[224,3584]{1,0:T(8,128)(2,1)} %wdec.1, ...), custom_call_target="tpu_custom_call" | custom-call | flops 900000000 | bytes 6000000 | tf_op jit(solution)/shard_map/pallas_call | solution.py:330
  55.9 1.8 %shard_map.93 = (f32[4,3584]{1,0:T(4,128)}, bf16[224,3584]{1,0:T(8,128)(2,1)}, f32[224,128]{1,0:T(8,128)}, f32[28,128]{1,0:T(8,128)}, f32[1,1]{1,0:T(1,128)}) custom-call(f32[4,3584]{1,0:T(4,128)S(1)} %get-tuple-element.15.recon, bf16[4,224,896]{2,1,0:T(8,128)(2,1)S(1)} %get-tuple-element.16.grad, f32[224,128]{1,0:T(8,128)S(1)} %get-tuple-element.17.code_grad, ...), custom_call_target="tpu_custom_call" | custom-call | tf_op jit(solution)/shard_map/pallas_call | solution.py:388

commit v4 on v3

--- a/solution.py
+++ b/solution.py
@@ -124,12 +124,18 @@
     norm_row = jnp.transpose(jnp.broadcast_to(norm_col, (LAT, 128)))[0:1, :]
 
     enc_load.wait()
-    for i in (1, 3, 2):
-        xx = (x + i) % NX
-        took(rg.at[xx], gsend.at[1], gx.at[xx]).wait_recv()
-    for kk in range(2):
+
+    def lay(kk):
         even, odd = rg[2 * kk].astype(F32), rg[2 * kk + 1].astype(F32)
         lhs[:, kk] = jnp.concatenate([even, odd], axis=1).astype(BF16)
+
+    beside_x = x + 1 - 2 * h
+    took(rg.at[beside_x], gsend.at[1], gx.at[beside_x]).wait_recv()
+    lay(k)
+    for kk in range(2):
+        xx = 2 * (1 - k) + kk
+        took(rg.at[xx], gsend.at[1], gx.at[xx]).wait_recv()
+    lay(1 - k)
     to_sib[0].wait_recv()
     to_sib[1].wait_recv()
     rows = lhs[...].reshape(ROWS, HALF)
@@ -261,7 +267,7 @@
     pbc[c] = pen
     push(pbc.at[c], pbc.at[c], pen_send.at[3], pen_recv.at[3], sib)
     sent.append(took(pbc.at[0], pen_send.at[3], pen_recv.at[3]))
-    for i in (2, 1, 3):
+    for i in (1, 3, 2):
         xx = (x + i) % NX
         took(err.at[c, xx], esend.at[1], ex.at[xx]).wait_recv()
         push(err.at[c, xx], err.at[c, xx], esend.at[2], es.at[xx], sib)
@@ -284,10 +290,11 @@
     cg = jnp.zeros((LAT, ROWS), F32)
     cg = quarter(c, h, cg)
     cg = quarter(c, 1 - h, cg)
-    for xx in range(4):
-        took(err.at[1 - c, xx], esend.at[2], es.at[xx]).wait_recv()
-    cg = quarter(1 - c, 0, cg)
-    cg = quarter(1 - c, 1, cg)
+    for hq in (1 - h, h):
+        for kk in range(2):
+            xx = 2 * kk + hq
+            took(err.at[1 - c, xx], esend.at[2], es.at[xx]).wait_recv()
+        cg = quarter(1 - c, hq, cg)
     cg_o[...] = cg + norm_col
 
     squares = jnp.zeros((8, Q), F32)

time: 57.8 us -> 57.4 us (level)
  no operation moved by 1% of the time
where the time goes in v4:
time: 57.4 us; the launch traced here: 57.2 us
  Pallas kernels  56.6 us (99%)
  between operations  0.64 us (1%)
    pallas_call x1, Pallas kernels, per_device(): pl.pallas_call(kernel, out_shape=(jax.ShapeDtypeStruct((4, D), F32), jax....  54.8 us
    pallas_call x1, Pallas kernels, per_device(): pl.pallas_call(write_out, out_shape=(jax.ShapeDtypeStruct((4, D), F32), j...  1.77 us

profile of v4, /device:TPU:1, one launch (start us, length us, event | category | flops | bytes accessed | tf_op | source)
XLA Modules:
  0.0 57.2 jit_solution(14101111191928452964)
XLA Ops:
  0.6 54.8 %shard_map.92 = (f32[4,3584]{1,0:T(4,128)S(1)}, bf16[4,224,896]{2,1,0:T(8,128)(2,1)S(1)}, f32[224,128]{1,0:T(8,128)S(1)}, f32[28,128]{1,0:T(8,128)S(1)}, f32[8,128]{1,0:T(8,128)S(1)}) custom-call(bf16[4,3584]{1,0:T(4,128)(2,1)} %resid.1, bf16[224,3584]{1,0:T(8,128)(2,1)} %wenc.1, f32[1,224]{1,0:T(1,128)} %bitcast.8, bf16[224,3584]{1,0:T(8,128)(2,1)} %wdec.1, ...), custom_call_target="tpu_custom_call" | custom-call | flops 900000000 | bytes 6000000 | tf_op jit(solution)/shard_map/pallas_call | solution.py:337
  55.5 1.8 %shard_map.93 = (f32[4,3584]{1,0:T(4,128)}, bf16[224,3584]{1,0:T(8,128)(2,1)}, f32[224,128]{1,0:T(8,128)}, f32[28,128]{1,0:T(8,128)}, f32[1,1]{1,0:T(1,128)}) custom-call(f32[4,3584]{1,0:T(4,128)S(1)} %get-tuple-element.15.recon, bf16[4,224,896]{2,1,0:T(8,128)(2,1)S(1)} %get-tuple-element.16.grad, f32[224,128]{1,0:T(8,128)S(1)} %get-tuple-element.17.code_grad, ...), custom_call_target="tpu_custom_call" | custom-call | tf_op jit(solution)/shard_map/pallas_call | solution.py:395

commit v5 on v4

--- a/solution.py
+++ b/solution.py
@@ -89,7 +89,7 @@
     own.wait()
     pl.semaphore_wait(barrier, len(partners))
 
-    for j in NEAR:
+    for j in FAR:
         push(rg.at[x, y], rg.at[x, y], gsend.at[0], gy.at[y], at_y(j))
     for i in (2, 1, 3):
         push(rg.at[x, y], rg.at[x, y], gsend.at[1], gx.at[x], at_x(i))

time: 57.4 us -> 58.3 us (1.016)
  Pallas kernels: 56.6 us -> 57.4 us
    pallas_call x1, Pallas kernels: 54.8 us -> 55.7 us  [per_device(): pl.pallas_call(kernel, out_shape=(jax.ShapeDtypeStruct((4, D), F32), jax....]
where the time goes in v5:
time: 58.3 us; the launch traced here: 58.1 us
  Pallas kernels  57.4 us (98%)
  between operations  0.64 us (1%)
    pallas_call x1, Pallas kernels, per_device(): pl.pallas_call(kernel, out_shape=(jax.ShapeDtypeStruct((4, D), F32), jax....  55.7 us
    pallas_call x1, Pallas kernels, per_device(): pl.pallas_call(write_out, out_shape=(jax.ShapeDtypeStruct((4, D), F32), j...  1.77 us

profile of v5, /device:TPU:1, one launch (start us, length us, event | category | flops | bytes accessed | tf_op | source)
XLA Modules:
  0.0 58.1 jit_solution(16747317707249781897)
XLA Ops:
  0.6 55.7 %shard_map.92 = (f32[4,3584]{1,0:T(4,128)S(1)}, bf16[4,224,896]{2,1,0:T(8,128)(2,1)S(1)}, f32[224,128]{1,0:T(8,128)S(1)}, f32[28,128]{1,0:T(8,128)S(1)}, f32[8,128]{1,0:T(8,128)S(1)}) custom-call(bf16[4,3584]{1,0:T(4,128)(2,1)} %resid.1, bf16[224,3584]{1,0:T(8,128)(2,1)} %wenc.1, f32[1,224]{1,0:T(1,128)} %bitcast.8, bf16[224,3584]{1,0:T(8,128)(2,1)} %wdec.1, ...), custom_call_target="tpu_custom_call" | custom-call | flops 900000000 | bytes 6000000 | tf_op jit(solution)/shard_map/pallas_call | solution.py:337
  56.3 1.8 %shard_map.93 = (f32[4,3584]{1,0:T(4,128)}, bf16[224,3584]{1,0:T(8,128)(2,1)}, f32[224,128]{1,0:T(8,128)}, f32[28,128]{1,0:T(8,128)}, f32[1,1]{1,0:T(1,128)}) custom-call(f32[4,3584]{1,0:T(4,128)S(1)} %get-tuple-element.15.recon, bf16[4,224,896]{2,1,0:T(8,128)(2,1)S(1)} %get-tuple-element.16.grad, f32[224,128]{1,0:T(8,128)S(1)} %get-tuple-element.17.code_grad, ...), custom_call_target="tpu_custom_call" | custom-call | tf_op jit(solution)/shard_map/pallas_call | solution.py:395
